TPU v7x, 128 devices: a whole 4x4x4 slice. The times are simulated.
128 devices in a mesh: comp: 4 (over x), cell: 32 (over y, z, core).
Axes of the slice: x: 4, y: 4, z: 4, core: 2. Of those that a mesh axis runs over, the one named last changes fastest.
Arguments:
- biomass: float32 [48, 64, 16384], P(None, None, ('comp', 'cell')), may hold values from 0.1 to 2
- patch_area: float32 [48, 16384], P(None, ('comp', 'cell')), may hold values from 0.005 to 0.04
- cohort_traits: float32 [4, 64], replicated, may hold values from 0.1 to 1
- cell_forcing: float32 [5, 16384], P(None, ('comp', 'cell')), may hold values from 0.1 to 1
- disturb_weight: float32 [4, 16384], P(None, ('comp', 'cell')), may hold values from 0 to 0.25
- transitions: float32 [4, 48, 48], replicated, may hold values from 0 to 1
- land_source: int32 [131072], P(('comp', 'cell')), may hold values from -1 to 127, as said below
- pair_share: float32 [131072], P(('comp', 'cell')), may hold values from 0.05 to 0.35
- river_target: int32 [131072], P(('comp', 'cell')), may hold values from -1 to 2047, as said below
- downstream_step: int32 [262144], P(('comp', 'cell')), may hold values from 0 to 2047
- river_water: float32 [4, 262144], P(None, ('comp', 'cell')), may hold values from 0.5 to 2
- river_rates: float32 [4, 262144], P(None, ('comp', 'cell')), may hold values from 0.05 to 0.8
- capacity: float32 [262144], P(('comp', 'cell')), may hold values from 0.5 to 5
Outputs:
- new_biomass: float32 [48, 64, 16384], P(None, None, ('comp', 'cell'))
- flooded: float32 [16384], P(('comp', 'cell'))
- river_state: float32 [4, 262144], P(None, ('comp', 'cell'))
Inputs may be any that keep to these rules, and one draw needn't show every extreme that they name: `land_source`: A device's list has one block of 8 rows for each receiving device, in comp+cell order; live rows come first in every block, padding rows hold -1. Every device has at least one full block, and one receiving device gets full blocks from every device. `river_target`: row s of block i on device j is live exactly when row s of block j on device i of land_source is live, and then names the receiving river cell of device j; padding rows hold -1.
All inputs are finite; a program needn't handle non-finite values.
Results may differ from a plain program's by a relative error of at most 0.0001.
Values sent between devices are 32-bit elements; how exact they have to be, the bound alone decides.
A program may use at most 64 MiB of HBM per device.

v0:
```python
import jax
import jax.numpy as jnp
from jax import lax
from jax.sharding import PartitionSpec as P

NSUB = 12
highest = lax.Precision.HIGHEST


def in_blocks(value, dim, devices):
    before, after = (value.shape[:dim], value.shape[dim + 1 :])
    return jnp.moveaxis(value.reshape(*before, devices, -1, *after), dim, 0)


def in_order(blocks, dim):
    blocks = jnp.moveaxis(blocks, 0, dim)
    lengths = blocks.shape
    return blocks.reshape(*lengths[:dim], lengths[dim] * lengths[dim + 1], *lengths[dim + 2 :])


def joined_exchange(value, axis, axes, splits, concats):
    sizes = [lax.axis_size(a) for a in axes]
    blocks = in_blocks(value, splits[0], sizes[0])
    blocks = jnp.moveaxis(in_blocks(blocks, splits[1] + 1, sizes[1]), 0, 1)
    inside = blocks.shape[2:]
    blocks = blocks.reshape(-1, *inside)
    blocks = lax.all_to_all(blocks, axis, split_axis=0, concat_axis=0, tiled=True)
    blocks = in_order(blocks.reshape(*sizes, *inside), concats[0] + 1)
    return in_order(blocks, concats[1])


def from_behind(value, axis, steps):
    count = lax.axis_size(axis)
    initial, last = (max(0, -steps), min(count, count - steps))
    return lax.ppermute(value, axis, [(source, source + steps) for source in range(initial, last)])


def canopy(biomass, patch_area, cohort_traits, cell_forcing):
    leaf_area = biomass * cohort_traits[0][None, :, None]
    bin_count = biomass.shape[1]
    taller_mask = (jnp.arange(bin_count)[None, :] > jnp.arange(bin_count)[:, None]).astype(
        jnp.float32
    )
    leaf_above = jnp.einsum("kj,pjc->pkc", taller_mask, leaf_area, precision=highest)
    light_level = cell_forcing[0]
    assimilation = (
        cohort_traits[1][None, :, None]
        * leaf_area
        * jnp.exp(-0.05 * leaf_above)
        * (light_level / (light_level + 0.5))[None, None, :]
    )
    transpiration = 0.5 * jnp.sum(patch_area * jnp.sum(assimilation, axis=1), axis=0)
    wet_rain = cell_forcing[1] * cell_forcing[2]
    runoff = jnp.stack(
        [
            wet_rain * (1.0 - cell_forcing[4]),
            wet_rain * cell_forcing[4],
            cell_forcing[3] * jnp.exp(-0.5 * transpiration),
        ]
    )
    grown_mass = biomass * (1.0 - 0.1 * cohort_traits[2])[None, :, None] + 0.5 * assimilation
    return (grown_mass, runoff)


def transit(grown_mass, disturb_weight, transitions):
    patches, bin_count, cell_count = grown_mass.shape
    flat_mass = grown_mass.reshape(patches, bin_count * cell_count)
    transited = jnp.zeros_like(grown_mass)
    for kind_index in range(transitions.shape[0]):
        moved_mass = jnp.dot(
            transitions[kind_index],
            flat_mass,
            precision=highest,
            preferred_element_type=jnp.float32,
        )
        transited = (
            transited
            + moved_mass.reshape(patches, bin_count, cell_count)
            * disturb_weight[kind_index][None, None, :]
        )
    return transited


def scatter_pair(outflow, slots, segments):
    return jax.ops.segment_sum(outflow.T, slots, num_segments=segments).T


def shards(
    biomass,
    patch_area,
    cohort_traits,
    cell_forcing,
    disturb_weight,
    transitions,
    land_source,
    pair_share,
    river_target,
    downstream_step,
    river_water,
    river_rates,
    capacity,
):
    land_cells = biomass.shape[2]
    rivers = river_water.shape[1]
    comp_parts = lax.axis_size("comp")
    grown_mass, runoff = canopy(biomass, patch_area, cohort_traits, cell_forcing)
    is_live = land_source >= 0
    safe_source = jnp.where(is_live, land_source, 0)
    pair_values = jnp.where(
        is_live[None, :], pair_share[None, :] * jnp.take(runoff, safe_source, axis=1), 0.0
    )
    arrived = joined_exchange(
        pair_values.reshape(3, comp_parts, -1), ("comp", "cell"), ("comp", "cell"), (1, 2), (1, 2)
    ).reshape(3, -1)
    transited = transit(grown_mass, disturb_weight, transitions)
    has_target = river_target >= 0
    safe_target = jnp.where(has_target, river_target, rivers)
    runoff_in = jax.ops.segment_sum(arrived.T, safe_target, num_segments=rivers + 1)[:rivers].T
    local_cell = jnp.arange(rivers, dtype=jnp.int32)
    down_slot = jnp.where(downstream_step > 0, local_cell + downstream_step, 2 * rivers)
    fraction = 1.0 / NSUB
    surface_in = fraction * runoff_in[0:2]
    deep_in = jnp.stack([fraction * runoff_in[2], jnp.zeros_like(runoff_in[2])])
    hill_rate = river_rates[0:2]
    channel_rate = river_rates[2:4]

    def substep(sub_index, state_pair):
        hill_water, channel = state_pair
        hill_out = hill_rate * hill_water
        outflow = channel_rate * channel
        spread = scatter_pair(outflow, down_slot, 2 * rivers + 1)
        from_above = from_behind(spread[:, rivers : 2 * rivers], ("comp", "cell"), 1)
        inflow = spread[:, :rivers] + from_above
        return (hill_water - hill_out + surface_in, channel - outflow + hill_out + inflow + deep_in)

    hill_water, channel = lax.fori_loop(0, NSUB, substep, (river_water[0:2], river_water[2:4]))
    stored_total = channel[0] + channel[1]
    inundation = stored_total / (stored_total + capacity)
    flood_back = jnp.where(has_target, inundation[jnp.where(has_target, river_target, 0)], 0.0)
    returned = lax.all_to_all(
        lax.all_to_all(
            flood_back.reshape(comp_parts, -1), "cell", split_axis=1, concat_axis=1, tiled=True
        ),
        "comp",
        split_axis=0,
        concat_axis=0,
        tiled=True,
    ).reshape(-1)
    flooded = jax.ops.segment_sum(
        pair_share * returned,
        jnp.where(is_live, land_source, land_cells),
        num_segments=land_cells + 1,
    )[:land_cells]
    new_biomass = transited * jnp.exp(-cohort_traits[3][None, :, None] * flooded[None, None, :])
    river_state = jnp.concatenate([hill_water, channel], axis=0)
    return (new_biomass, flooded, river_state)


def solution(mesh):
    return jax.shard_map(
        shards,
        mesh=mesh,
        in_specs=(
            P(None, None, ("comp", "cell")),
            P(None, ("comp", "cell")),
            P(),
            P(None, ("comp", "cell")),
            P(None, ("comp", "cell")),
            P(),
            P(("comp", "cell")),
            P(("comp", "cell")),
            P(("comp", "cell")),
            P(("comp", "cell")),
            P(None, ("comp", "cell")),
            P(None, ("comp", "cell")),
            P(("comp", "cell")),
        ),
        out_specs=(P(None, None, ("comp", "cell")), P(("comp", "cell")), P(None, ("comp", "cell"))),
        check_vma=False,
    )
```

profile of v0, /device:TPU:8, one launch (start us, length us, event | category | flops | bytes accessed | tf_op | source)
XLA Modules:
  0.0 398.8 jit_solution(263364392975987532)
XLA Ops:
  12.3 10.5 %all-to-all-start = ((f32[128,3,1,8]{3,2,1,0:T(1,128)}), f32[128,3,1,8]{3,2,1,0:T(1,128)S(1)}, u32[]{:S(2)}, u32[]{:S(2)}) async-start(f32[128,3,1,8]{3,2,1,0:T(1,128)} %bitcast.27), calls=%async_computation | async-start | bytes 393216 | tf_op jit(solution)/shard_map/all_to_all | solution.py:27
  22.8 3.7 fusion.18
  26.5 3.6 fusion.21
  30.3 3.7 fusion.24
  39.1 6.5 %scatter_custom_fusion.1 = f32[2049,3]{1,0:T(8,128)S(1)} fusion(s32[1024]{0:T(1024)S(1)} %get-tuple-element.76, f32[1024,3]{1,0:T(8,128)S(1)} %copy.88, f32[]{:T(128)} %constant.23.clone.1), kind=kCustom, calls=%fused_computation.45 | custom fusion | flops 3072 | bytes 24592 | tf_op jit(solution)/shard_map/scatter-add | solution.py:118
  48.2 300.2 %while.12 = (s32[]{:T(128)}, f32[2,2048]{0,1:T(8,128)}, f32[2,2048]{0,1:T(8,128)S(1)}, f32[2,2048]{0,1:T(8,128)}, f32[2,2048]{0,1:T(8,128)}, /*index=5*/f32[2,20...) while((s32[]{:T(128)}, f32[2,2048]{0,1:T(8,128)}, f32[2,2048]{0,1:T(8,128)S(1)}, ...), condition=%wide.region_5.6_spmd, body=%wide.region_3.5_spmd.sunk | while | flops 45058 | bytes 1851629 | solution.py:136
  48.2 12.4 %scatter_custom_fusion.9 = f32[4097,2]{1,0:T(8,128)S(1)} fusion(s32[2048]{0:T(1024)S(1)} %get-tuple-element.177, f32[]{:T(128)} %constant.23.clone.1..sunk, f32[2,2048]{0,1:T(8,128)} %get-tuple-element.176, f32[2,2048]{0,1:T(8,128)S(1)} %get-tuple-element.163), kind=kCustom, calls=%fused_computation.5.clone.1 | custom fusion | flops 8192 | bytes 1097740 | tf_op jit(solution)/shard_map/while/body/eval_jaxpr/scatter-add | solution.py:85
  72.5 12.4 %scatter_custom_fusion.9 = f32[4097,2]{1,0:T(8,128)S(1)} fusion(s32[2048]{0:T(1024)S(1)} %get-tuple-element.177, f32[]{:T(128)} %constant.23.clone.1..sunk, f32[2,2048]{0,1:T(8,128)} %get-tuple-element.176, f32[2,2048]{0,1:T(8,128)S(1)} %get-tuple-element.163), kind=kCustom, calls=%fused_computation.5.clone.1 | custom fusion | flops 8192 | bytes 1097740 | tf_op jit(solution)/shard_map/while/body/eval_jaxpr/scatter-add | solution.py:85
  98.3 12.4 %scatter_custom_fusion.9 = f32[4097,2]{1,0:T(8,128)S(1)} fusion(s32[2048]{0:T(1024)S(1)} %get-tuple-element.177, f32[]{:T(128)} %constant.23.clone.1..sunk, f32[2,2048]{0,1:T(8,128)} %get-tuple-element.176, f32[2,2048]{0,1:T(8,128)S(1)} %get-tuple-element.163), kind=kCustom, calls=%fused_computation.5.clone.1 | custom fusion | flops 8192 | bytes 1097740 | tf_op jit(solution)/shard_map/while/body/eval_jaxpr/scatter-add | solution.py:85
  122.7 12.4 %scatter_custom_fusion.9 = f32[4097,2]{1,0:T(8,128)S(1)} fusion(s32[2048]{0:T(1024)S(1)} %get-tuple-element.177, f32[]{:T(128)} %constant.23.clone.1..sunk, f32[2,2048]{0,1:T(8,128)} %get-tuple-element.176, f32[2,2048]{0,1:T(8,128)S(1)} %get-tuple-element.163), kind=kCustom, calls=%fused_computation.5.clone.1 | custom fusion | flops 8192 | bytes 1097740 | tf_op jit(solution)/shard_map/while/body/eval_jaxpr/scatter-add | solution.py:85
  148.6 12.4 %scatter_custom_fusion.9 = f32[4097,2]{1,0:T(8,128)S(1)} fusion(s32[2048]{0:T(1024)S(1)} %get-tuple-element.177, f32[]{:T(128)} %constant.23.clone.1..sunk, f32[2,2048]{0,1:T(8,128)} %get-tuple-element.176, f32[2,2048]{0,1:T(8,128)S(1)} %get-tuple-element.163), kind=kCustom, calls=%fused_computation.5.clone.1 | custom fusion | flops 8192 | bytes 1097740 | tf_op jit(solution)/shard_map/while/body/eval_jaxpr/scatter-add | solution.py:85
  173.0 12.4 %scatter_custom_fusion.9 = f32[4097,2]{1,0:T(8,128)S(1)} fusion(s32[2048]{0:T(1024)S(1)} %get-tuple-element.177, f32[]{:T(128)} %constant.23.clone.1..sunk, f32[2,2048]{0,1:T(8,128)} %get-tuple-element.176, f32[2,2048]{0,1:T(8,128)S(1)} %get-tuple-element.163), kind=kCustom, calls=%fused_computation.5.clone.1 | custom fusion | flops 8192 | bytes 1097740 | tf_op jit(solution)/shard_map/while/body/eval_jaxpr/scatter-add | solution.py:85
  198.6 12.4 %scatter_custom_fusion.9 = f32[4097,2]{1,0:T(8,128)S(1)} fusion(s32[2048]{0:T(1024)S(1)} %get-tuple-element.177, f32[]{:T(128)} %constant.23.clone.1..sunk, f32[2,2048]{0,1:T(8,128)} %get-tuple-element.176, f32[2,2048]{0,1:T(8,128)S(1)} %get-tuple-element.163), kind=kCustom, calls=%fused_computation.5.clone.1 | custom fusion | flops 8192 | bytes 1097740 | tf_op jit(solution)/shard_map/while/body/eval_jaxpr/scatter-add | solution.py:85
  222.9 12.4 %scatter_custom_fusion.9 = f32[4097,2]{1,0:T(8,128)S(1)} fusion(s32[2048]{0:T(1024)S(1)} %get-tuple-element.177, f32[]{:T(128)} %constant.23.clone.1..sunk, f32[2,2048]{0,1:T(8,128)} %get-tuple-element.176, f32[2,2048]{0,1:T(8,128)S(1)} %get-tuple-element.163), kind=kCustom, calls=%fused_computation.5.clone.1 | custom fusion | flops 8192 | bytes 1097740 | tf_op jit(solution)/shard_map/while/body/eval_jaxpr/scatter-add | solution.py:85
  247.9 12.4 %scatter_custom_fusion.9 = f32[4097,2]{1,0:T(8,128)S(1)} fusion(s32[2048]{0:T(1024)S(1)} %get-tuple-element.177, f32[]{:T(128)} %constant.23.clone.1..sunk, f32[2,2048]{0,1:T(8,128)} %get-tuple-element.176, f32[2,2048]{0,1:T(8,128)S(1)} %get-tuple-element.163), kind=kCustom, calls=%fused_computation.5.clone.1 | custom fusion | flops 8192 | bytes 1097740 | tf_op jit(solution)/shard_map/while/body/eval_jaxpr/scatter-add | solution.py:85
  272.2 12.4 %scatter_custom_fusion.9 = f32[4097,2]{1,0:T(8,128)S(1)} fusion(s32[2048]{0:T(1024)S(1)} %get-tuple-element.177, f32[]{:T(128)} %constant.23.clone.1..sunk, f32[2,2048]{0,1:T(8,128)} %get-tuple-element.176, f32[2,2048]{0,1:T(8,128)S(1)} %get-tuple-element.163), kind=kCustom, calls=%fused_computation.5.clone.1 | custom fusion | flops 8192 | bytes 1097740 | tf_op jit(solution)/shard_map/while/body/eval_jaxpr/scatter-add | solution.py:85
  298.1 12.4 %scatter_custom_fusion.9 = f32[4097,2]{1,0:T(8,128)S(1)} fusion(s32[2048]{0:T(1024)S(1)} %get-tuple-element.177, f32[]{:T(128)} %constant.23.clone.1..sunk, f32[2,2048]{0,1:T(8,128)} %get-tuple-element.176, f32[2,2048]{0,1:T(8,128)S(1)} %get-tuple-element.163), kind=kCustom, calls=%fused_computation.5.clone.1 | custom fusion | flops 8192 | bytes 1097740 | tf_op jit(solution)/shard_map/while/body/eval_jaxpr/scatter-add | solution.py:85
  322.5 12.4 %scatter_custom_fusion.9 = f32[4097,2]{1,0:T(8,128)S(1)} fusion(s32[2048]{0:T(1024)S(1)} %get-tuple-element.177, f32[]{:T(128)} %constant.23.clone.1..sunk, f32[2,2048]{0,1:T(8,128)} %get-tuple-element.176, f32[2,2048]{0,1:T(8,128)S(1)} %get-tuple-element.163), kind=kCustom, calls=%fused_computation.5.clone.1 | custom fusion | flops 8192 | bytes 1097740 | tf_op jit(solution)/shard_map/while/body/eval_jaxpr/scatter-add | solution.py:85
  349.1 6.2 %gather_fusion.1 = f32[1024]{0:T(1024)S(1)} fusion(f32[2048]{0:T(1024)S(1)} %add_divide_fusion, s32[1024]{0:T(1024)S(1)} %get-tuple-element.75), kind=kCustom, calls=%fused_computation.1 | custom fusion | bytes 12288 | tf_op jit(solution)/shard_map/gather | solution.py:139
  356.0 10.4 %all-to-all-start.1 = ((f32[4,32,8]{2,0,1:T(4,128)}), f32[4,32,8]{2,0,1:T(4,128)S(1)}, u32[]{:S(2)}, u32[]{:S(2)}) async-start(f32[4,32,8]{2,0,1:T(4,128)} %copy.90), calls=%async_computation.1 | async-start | bytes 131072 | tf_op jit(solution)/shard_map/all_to_all | solution.py:141
  376.9 4.0 all-to-all-start.2
  381.5 4.7 %all-to-all-done.2 = f32[4,1,256]{2,1,0:T(1,128)S(1)} async-done(((f32[4,1,256]{2,1,0:T(1,128)}), f32[4,1,256]{2,1,0:T(1,128)S(1)}, u32[]{:S(2)}, u32[]{:S(2)}) %all-to-all-start.2) | async-done | bytes 4128 | tf_op jit(solution)/shard_map/all_to_all | solution.py:140
  386.2 7.6 %scatter_custom_fusion.2 = f32[129]{0:T(256)S(1)} fusion(s32[1024]{0:T(1024)S(1)} %get-tuple-element.80, f32[1024]{0:T(1024)S(1)} %mul.247, f32[]{:T(128)} %constant.23.clone.1), kind=kCustom, calls=%fused_computation.78 | custom fusion | flops 1024 | bytes 520 | tf_op jit(solution)/shard_map/scatter-add | solution.py:149
  393.9 4.9 %fusion.5 = f32[48,64,128]{2,1,0:T(8,128)} fusion(f32[6,8,64,128]{3,2,1,0:T(8,128)} %copy.104, f32[6,8,64,128]{3,2,1,0:T(8,128)} %copy.103, f32[6,8,64,128]{3,2,1,0:T(8,128)} %copy.102, f32[6,8,64,128]{3,2,1,0:T(8,128)} %copy.101, f32[64,128]{1,0:T(8,128)S(1)} %multiply_exponential_fusion, f32[128]{0:T(128)S(1)} %get-tuple-element.86, ...), kind=kLoop, calls=%fused_computation.14 | loop fusion | flops 3145728 | bytes 7899136 | tf_op jit(solution)/shard_map/mul | solution.py:154
  (291 shorter events, 182.5 us)
Async XLA Ops:
  7.2 23.1 %copy-start.4 = (f32[48,64,128]{2,1,0:T(8,128)}, f32[48,64,128]{2,1,0:T(8,128)S(1)}, u32[]{:S(2)}) copy-start(f32[48,64,128]{2,1,0:T(8,128)S(1)} %get-tuple-element.70) | copy-start | bytes 4718596
  7.2 15.6 %copy-start.9 = (f32[4,48,48]{2,1,0:T(8,128)S(1)}, f32[4,48,48]{2,1,0:T(8,128)}, u32[]{:S(2)}) copy-start(f32[4,48,48]{2,1,0:T(8,128)} %param.20) | copy-start | bytes 110596
  12.3 26.1 %all-to-all-start = ((f32[128,3,1,8]{3,2,1,0:T(1,128)}), f32[128,3,1,8]{3,2,1,0:T(1,128)S(1)}, u32[]{:S(2)}, u32[]{:S(2)}) async-start(f32[128,3,1,8]{3,2,1,0:T(1,128)} %bitcast.27), calls=%async_computation | async-start | bytes 393216 | tf_op jit(solution)/shard_map/all_to_all | solution.py:27
  63.6 7.8 %collective-permute-start = (f32[2,2048]{1,0:T(2,128)S(1)}, f32[2,2048]{1,0:T(2,128)S(1)}, u32[]{:S(2)}, u32[]{:S(2)}) collective-permute-start(f32[2,2048]{1,0:T(2,128)S(1)} %copy.127), channel_id=1, source_target_pairs={{0,1},{1,2},{2,3},{3,4},{4,5},{5,6},{6,7},{7,8},{8,9},{9,10},{10,1... | collective-permute-start | bytes 49160 | tf_op jit(solution)/shard_map/while/body/eval_jaxpr/ppermute | solution.py:35
  86.4 5.2 %copy-start = (f32[2,2048]{0,1:T(8,128)S(1)}, f32[2,2048]{0,1:T(8,128)}, u32[]{:S(2)}) copy-start(f32[2,2048]{0,1:T(8,128)} %get-tuple-element.176) | copy-start | bytes 49156 | tf_op jit(solution)/shard_map/while
  88.0 9.3 %collective-permute-start = (f32[2,2048]{1,0:T(2,128)S(1)}, f32[2,2048]{1,0:T(2,128)S(1)}, u32[]{:S(2)}, u32[]{:S(2)}) collective-permute-start(f32[2,2048]{1,0:T(2,128)S(1)} %copy.127), channel_id=1, source_target_pairs={{0,1},{1,2},{2,3},{3,4},{4,5},{5,6},{6,7},{7,8},{8,9},{9,10},{10,1... | collective-permute-start | bytes 49160 | tf_op jit(solution)/shard_map/while/body/eval_jaxpr/ppermute | solution.py:35
  113.8 7.9 %collective-permute-start = (f32[2,2048]{1,0:T(2,128)S(1)}, f32[2,2048]{1,0:T(2,128)S(1)}, u32[]{:S(2)}, u32[]{:S(2)}) collective-permute-start(f32[2,2048]{1,0:T(2,128)S(1)} %copy.127), channel_id=1, source_target_pairs={{0,1},{1,2},{2,3},{3,4},{4,5},{5,6},{6,7},{7,8},{8,9},{9,10},{10,1... | collective-permute-start | bytes 49160 | tf_op jit(solution)/shard_map/while/body/eval_jaxpr/ppermute | solution.py:35
  136.6 5.3 %copy-start = (f32[2,2048]{0,1:T(8,128)S(1)}, f32[2,2048]{0,1:T(8,128)}, u32[]{:S(2)}) copy-start(f32[2,2048]{0,1:T(8,128)} %get-tuple-element.176) | copy-start | bytes 49156 | tf_op jit(solution)/shard_map/while
  138.2 9.4 %collective-permute-start = (f32[2,2048]{1,0:T(2,128)S(1)}, f32[2,2048]{1,0:T(2,128)S(1)}, u32[]{:S(2)}, u32[]{:S(2)}) collective-permute-start(f32[2,2048]{1,0:T(2,128)S(1)} %copy.127), channel_id=1, source_target_pairs={{0,1},{1,2},{2,3},{3,4},{4,5},{5,6},{6,7},{7,8},{8,9},{9,10},{10,1... | collective-permute-start | bytes 49160 | tf_op jit(solution)/shard_map/while/body/eval_jaxpr/ppermute | solution.py:35
  164.1 7.9 %collective-permute-start = (f32[2,2048]{1,0:T(2,128)S(1)}, f32[2,2048]{1,0:T(2,128)S(1)}, u32[]{:S(2)}, u32[]{:S(2)}) collective-permute-start(f32[2,2048]{1,0:T(2,128)S(1)} %copy.127), channel_id=1, source_target_pairs={{0,1},{1,2},{2,3},{3,4},{4,5},{5,6},{6,7},{7,8},{8,9},{9,10},{10,1... | collective-permute-start | bytes 49160 | tf_op jit(solution)/shard_map/while/body/eval_jaxpr/ppermute | solution.py:35
  186.8 5.0 %copy-start = (f32[2,2048]{0,1:T(8,128)S(1)}, f32[2,2048]{0,1:T(8,128)}, u32[]{:S(2)}) copy-start(f32[2,2048]{0,1:T(8,128)} %get-tuple-element.176) | copy-start | bytes 49156 | tf_op jit(solution)/shard_map/while
  188.5 9.1 %collective-permute-start = (f32[2,2048]{1,0:T(2,128)S(1)}, f32[2,2048]{1,0:T(2,128)S(1)}, u32[]{:S(2)}, u32[]{:S(2)}) collective-permute-start(f32[2,2048]{1,0:T(2,128)S(1)} %copy.127), channel_id=1, source_target_pairs={{0,1},{1,2},{2,3},{3,4},{4,5},{5,6},{6,7},{7,8},{8,9},{9,10},{10,1... | collective-permute-start | bytes 49160 | tf_op jit(solution)/shard_map/while/body/eval_jaxpr/ppermute | solution.py:35
  214.1 7.8 %collective-permute-start = (f32[2,2048]{1,0:T(2,128)S(1)}, f32[2,2048]{1,0:T(2,128)S(1)}, u32[]{:S(2)}, u32[]{:S(2)}) collective-permute-start(f32[2,2048]{1,0:T(2,128)S(1)} %copy.127), channel_id=1, source_target_pairs={{0,1},{1,2},{2,3},{3,4},{4,5},{5,6},{6,7},{7,8},{8,9},{9,10},{10,1... | collective-permute-start | bytes 49160 | tf_op jit(solution)/shard_map/while/body/eval_jaxpr/ppermute | solution.py:35
  238.4 8.4 %collective-permute-start = (f32[2,2048]{1,0:T(2,128)S(1)}, f32[2,2048]{1,0:T(2,128)S(1)}, u32[]{:S(2)}, u32[]{:S(2)}) collective-permute-start(f32[2,2048]{1,0:T(2,128)S(1)} %copy.127), channel_id=1, source_target_pairs={{0,1},{1,2},{2,3},{3,4},{4,5},{5,6},{6,7},{7,8},{8,9},{9,10},{10,1... | collective-permute-start | bytes 49160 | tf_op jit(solution)/shard_map/while/body/eval_jaxpr/ppermute | solution.py:35
  263.4 7.9 %collective-permute-start = (f32[2,2048]{1,0:T(2,128)S(1)}, f32[2,2048]{1,0:T(2,128)S(1)}, u32[]{:S(2)}, u32[]{:S(2)}) collective-permute-start(f32[2,2048]{1,0:T(2,128)S(1)} %copy.127), channel_id=1, source_target_pairs={{0,1},{1,2},{2,3},{3,4},{4,5},{5,6},{6,7},{7,8},{8,9},{9,10},{10,1... | collective-permute-start | bytes 49160 | tf_op jit(solution)/shard_map/while/body/eval_jaxpr/ppermute | solution.py:35
  286.1 5.2 %copy-start = (f32[2,2048]{0,1:T(8,128)S(1)}, f32[2,2048]{0,1:T(8,128)}, u32[]{:S(2)}) copy-start(f32[2,2048]{0,1:T(8,128)} %get-tuple-element.176) | copy-start | bytes 49156 | tf_op jit(solution)/shard_map/while
  287.7 9.4 %collective-permute-start = (f32[2,2048]{1,0:T(2,128)S(1)}, f32[2,2048]{1,0:T(2,128)S(1)}, u32[]{:S(2)}, u32[]{:S(2)}) collective-permute-start(f32[2,2048]{1,0:T(2,128)S(1)} %copy.127), channel_id=1, source_target_pairs={{0,1},{1,2},{2,3},{3,4},{4,5},{5,6},{6,7},{7,8},{8,9},{9,10},{10,1... | collective-permute-start | bytes 49160 | tf_op jit(solution)/shard_map/while/body/eval_jaxpr/ppermute | solution.py:35
  313.6 7.8 %collective-permute-start = (f32[2,2048]{1,0:T(2,128)S(1)}, f32[2,2048]{1,0:T(2,128)S(1)}, u32[]{:S(2)}, u32[]{:S(2)}) collective-permute-start(f32[2,2048]{1,0:T(2,128)S(1)} %copy.127), channel_id=1, source_target_pairs={{0,1},{1,2},{2,3},{3,4},{4,5},{5,6},{6,7},{7,8},{8,9},{9,10},{10,1... | collective-permute-start | bytes 49160 | tf_op jit(solution)/shard_map/while/body/eval_jaxpr/ppermute | solution.py:35
  336.3 5.3 %copy-start = (f32[2,2048]{0,1:T(8,128)S(1)}, f32[2,2048]{0,1:T(8,128)}, u32[]{:S(2)}) copy-start(f32[2,2048]{0,1:T(8,128)} %get-tuple-element.176) | copy-start | bytes 49156 | tf_op jit(solution)/shard_map/while
  338.0 9.4 %collective-permute-start = (f32[2,2048]{1,0:T(2,128)S(1)}, f32[2,2048]{1,0:T(2,128)S(1)}, u32[]{:S(2)}, u32[]{:S(2)}) collective-permute-start(f32[2,2048]{1,0:T(2,128)S(1)} %copy.127), channel_id=1, source_target_pairs={{0,1},{1,2},{2,3},{3,4},{4,5},{5,6},{6,7},{7,8},{8,9},{9,10},{10,1... | collective-permute-start | bytes 49160 | tf_op jit(solution)/shard_map/while/body/eval_jaxpr/ppermute | solution.py:35
  349.1 17.3 %copy-start.5 = (f32[48,64,128]{2,1,0:T(8,128)S(1)}, f32[48,64,128]{2,1,0:T(8,128)}, u32[]{:S(2)}) copy-start(f32[48,64,128]{2,1,0:T(8,128)} %copy-done.4) | copy-start | bytes 4718596
  356.0 20.2 %all-to-all-start.1 = ((f32[4,32,8]{2,0,1:T(4,128)}), f32[4,32,8]{2,0,1:T(4,128)S(1)}, u32[]{:S(2)}, u32[]{:S(2)}) async-start(f32[4,32,8]{2,0,1:T(4,128)} %copy.90), calls=%async_computation.1 | async-start | bytes 131072 | tf_op jit(solution)/shard_map/all_to_all | solution.py:141
  376.9 9.2 %all-to-all-start.2 = ((f32[4,1,256]{2,1,0:T(1,128)}), f32[4,1,256]{2,1,0:T(1,128)S(1)}, u32[]{:S(2)}, u32[]{:S(2)}) async-start(f32[4,1,256]{2,1,0:T(1,128)} %all_to_all.20), calls=%async_computation.2 | async-start | bytes 8192 | tf_op jit(solution)/shard_map/all_to_all | solution.py:140
  393.8 5.0 %copy-start.19 = (f32[128]{0:T(128)}, f32[128]{0:T(128)S(1)}, u32[]{:S(2)}) copy-start(f32[128]{0:T(128)S(1)} %slice.114) | copy-start | bytes 1540
  (44 other events, 103.6 us)
where the time goes:
time: 401 us; the launch traced here: 399 us
  other arithmetic  217 us (54%)
  local copies, waits for them, and re-layouts  101 us (25%)
  starting transfers between devices  57.4 us (14%)
  matrix products  17.1 us (4%)
  waiting for transfers between devices  4.7 us (1%)
    scatter-add x12, other arithmetic, scatter_pair(): return jax.ops.segment_sum(outflow.T, slots, num_segments=segments).T  149 us
    add x12, other arithmetic, substep(): hill_water - hill_out + surface_in  41.2 us
    slice x24, local copies, waits for them, and re-layouts, substep(): from_above = from_behind(spread[:, rivers:2 * rivers], ('comp', 'cell'), 1)  36.8 us
    ppermute x12, starting transfers between devices, from_behind(): lax.ppermute(value, axis, [(source, source + steps) for source in range(i...  32.6 us
    sub x12, local copies, waits for them, and re-layouts, substep(): channel - outflow + hill_out + inflow + deep_in  19.7 us
    dot_general x4, matrix products, transit(): jnp.dot(transitions[kind_index], flat_mass, precision=highest, preferred_...  13.5 us
    unnamed x42, local copies, waits for them, and re-layouts  11.2 us
    all_to_all x1, starting transfers between devices, joined_exchange(): lax.all_to_all(blocks, axis, split_axis=0, concat_axis=0, tiled=True)  10.5 us
  transfers between devices with their start and end apart: 15, of which 1 were waited for; matrix products, arithmetic and copies ran while one was open for 24% of the time, Pallas kernels for 0%

commit v1 on v0

--- a/solution.py
+++ b/solution.py
@@ -138,8 +138,16 @@
     inundation = stored_total / (stored_total + capacity)
     flood_back = jnp.where(has_target, inundation[jnp.where(has_target, river_target, 0)], 0.0)
     returned = lax.all_to_all(
-        lax.all_to_all(
-            flood_back.reshape(comp_parts, -1), "cell", split_axis=1, concat_axis=1, tiled=True
+        jnp.concatenate(
+            lax.all_to_all(
+                jnp.stack(
+                    jnp.split(flood_back.reshape(comp_parts, -1), lax.axis_size("cell"), axis=1)
+                ),
+                "cell",
+                0,
+                0,
+            ),
+            axis=1,
         ),
         "comp",
         split_axis=0,

time: 401 us -> 420 us (1.047)
  local copies, waits for them, and re-layouts: 101 us -> 121 us
    unnamed x42 -> x75, local copies, waits for them, and re-layouts: 11.2 us -> 31.3 us
  transfers between devices with their start and end apart: 15 -> 15, of which waited for: 1 -> 1; matrix products, arithmetic and copies ran while one was open for 24% -> 23% of each run, Pallas kernels for 0% -> 0%
where the time goes in v1:
time: 420 us; the launch traced here: 417 us
  other arithmetic  216 us (51%)
  local copies, waits for them, and re-layouts  121 us (29%)
  starting transfers between devices  57.4 us (14%)
  matrix products  17.1 us (4%)
  waiting for transfers between devices  4.7 us (1%)
    scatter-add x12, other arithmetic, scatter_pair(): return jax.ops.segment_sum(outflow.T, slots, num_segments=segments).T  149 us
    add x12, other arithmetic, substep(): hill_water - hill_out + surface_in  41.2 us
    slice x24, local copies, waits for them, and re-layouts, substep(): from_above = from_behind(spread[:, rivers:2 * rivers], ('comp', 'cell'), 1)  36.8 us
    ppermute x12, starting transfers between devices, from_behind(): lax.ppermute(value, axis, [(source, source + steps) for source in range(i...  32.6 us
    unnamed x75, local copies, waits for them, and re-layouts  31.3 us
    sub x12, local copies, waits for them, and re-layouts, substep(): channel - outflow + hill_out + inflow + deep_in  19.7 us
    dot_general x4, matrix products, transit(): jnp.dot(transitions[kind_index], flat_mass, precision=highest, preferred_...  13.5 us
    all_to_all x1, starting transfers between devices, joined_exchange(): lax.all_to_all(blocks, axis, split_axis=0, concat_axis=0, tiled=True)  10.5 us
  transfers between devices with their start and end apart: 15, of which 1 were waited for; matrix products, arithmetic and copies ran while one was open for 23% of the time, Pallas kernels for 0%

profile of v1, /device:TPU:8, one launch (start us, length us, event | category | flops | bytes accessed | tf_op | source)
XLA Modules:
  0.0 417.5 jit_solution(5937459440676506805)
XLA Ops:
  11.0 10.5 %all-to-all-start = ((f32[128,3,1,8]{3,2,1,0:T(1,128)}), f32[128,3,1,8]{3,2,1,0:T(1,128)S(1)}, u32[]{:S(2)}, u32[]{:S(2)}) async-start(f32[128,3,1,8]{3,2,1,0:T(1,128)} %bitcast.27), calls=%async_computation | async-start | bytes 393216 | tf_op jit(solution)/shard_map/all_to_all | solution.py:27
  21.5 3.7 fusion.18
  25.2 3.6 fusion.21
  28.9 3.7 fusion.24
  37.8 6.5 %scatter_custom_fusion.1 = f32[2049,3]{1,0:T(8,128)S(1)} fusion(s32[1024]{0:T(1024)S(1)} %get-tuple-element.76, f32[1024,3]{1,0:T(8,128)S(1)} %copy.254, f32[]{:T(128)} %constant.23.clone.1), kind=kCustom, calls=%fused_computation.45 | custom fusion | flops 3072 | bytes 24592 | tf_op jit(solution)/shard_map/scatter-add | solution.py:118
  46.8 300.2 %while.12 = (s32[]{:T(128)}, f32[2,2048]{0,1:T(8,128)}, f32[2,2048]{0,1:T(8,128)S(1)}, f32[2,2048]{0,1:T(8,128)}, f32[2,2048]{0,1:T(8,128)}, /*index=5*/f32[2,20...) while((s32[]{:T(128)}, f32[2,2048]{0,1:T(8,128)}, f32[2,2048]{0,1:T(8,128)S(1)}, ...), condition=%wide.region_5.6_spmd, body=%wide.region_3.5_spmd.sunk | while | flops 45058 | bytes 1851629 | solution.py:136
  46.8 12.4 %scatter_custom_fusion.9 = f32[4097,2]{1,0:T(8,128)S(1)} fusion(s32[2048]{0:T(1024)S(1)} %get-tuple-element.179, f32[]{:T(128)} %constant.23.clone.1..sunk, f32[2,2048]{0,1:T(8,128)} %get-tuple-element.178, f32[2,2048]{0,1:T(8,128)S(1)} %get-tuple-element.165), kind=kCustom, calls=%fused_computation.5.clone.1 | custom fusion | flops 8192 | bytes 1097740 | tf_op jit(solution)/shard_map/while/body/eval_jaxpr/scatter-add | solution.py:85
  71.2 12.4 %scatter_custom_fusion.9 = f32[4097,2]{1,0:T(8,128)S(1)} fusion(s32[2048]{0:T(1024)S(1)} %get-tuple-element.179, f32[]{:T(128)} %constant.23.clone.1..sunk, f32[2,2048]{0,1:T(8,128)} %get-tuple-element.178, f32[2,2048]{0,1:T(8,128)S(1)} %get-tuple-element.165), kind=kCustom, calls=%fused_computation.5.clone.1 | custom fusion | flops 8192 | bytes 1097740 | tf_op jit(solution)/shard_map/while/body/eval_jaxpr/scatter-add | solution.py:85
  97.0 12.4 %scatter_custom_fusion.9 = f32[4097,2]{1,0:T(8,128)S(1)} fusion(s32[2048]{0:T(1024)S(1)} %get-tuple-element.179, f32[]{:T(128)} %constant.23.clone.1..sunk, f32[2,2048]{0,1:T(8,128)} %get-tuple-element.178, f32[2,2048]{0,1:T(8,128)S(1)} %get-tuple-element.165), kind=kCustom, calls=%fused_computation.5.clone.1 | custom fusion | flops 8192 | bytes 1097740 | tf_op jit(solution)/shard_map/while/body/eval_jaxpr/scatter-add | solution.py:85
  121.4 12.4 %scatter_custom_fusion.9 = f32[4097,2]{1,0:T(8,128)S(1)} fusion(s32[2048]{0:T(1024)S(1)} %get-tuple-element.179, f32[]{:T(128)} %constant.23.clone.1..sunk, f32[2,2048]{0,1:T(8,128)} %get-tuple-element.178, f32[2,2048]{0,1:T(8,128)S(1)} %get-tuple-element.165), kind=kCustom, calls=%fused_computation.5.clone.1 | custom fusion | flops 8192 | bytes 1097740 | tf_op jit(solution)/shard_map/while/body/eval_jaxpr/scatter-add | solution.py:85
  147.3 12.4 %scatter_custom_fusion.9 = f32[4097,2]{1,0:T(8,128)S(1)} fusion(s32[2048]{0:T(1024)S(1)} %get-tuple-element.179, f32[]{:T(128)} %constant.23.clone.1..sunk, f32[2,2048]{0,1:T(8,128)} %get-tuple-element.178, f32[2,2048]{0,1:T(8,128)S(1)} %get-tuple-element.165), kind=kCustom, calls=%fused_computation.5.clone.1 | custom fusion | flops 8192 | bytes 1097740 | tf_op jit(solution)/shard_map/while/body/eval_jaxpr/scatter-add | solution.py:85
  171.6 12.4 %scatter_custom_fusion.9 = f32[4097,2]{1,0:T(8,128)S(1)} fusion(s32[2048]{0:T(1024)S(1)} %get-tuple-element.179, f32[]{:T(128)} %constant.23.clone.1..sunk, f32[2,2048]{0,1:T(8,128)} %get-tuple-element.178, f32[2,2048]{0,1:T(8,128)S(1)} %get-tuple-element.165), kind=kCustom, calls=%fused_computation.5.clone.1 | custom fusion | flops 8192 | bytes 1097740 | tf_op jit(solution)/shard_map/while/body/eval_jaxpr/scatter-add | solution.py:85
  197.2 12.4 %scatter_custom_fusion.9 = f32[4097,2]{1,0:T(8,128)S(1)} fusion(s32[2048]{0:T(1024)S(1)} %get-tuple-element.179, f32[]{:T(128)} %constant.23.clone.1..sunk, f32[2,2048]{0,1:T(8,128)} %get-tuple-element.178, f32[2,2048]{0,1:T(8,128)S(1)} %get-tuple-element.165), kind=kCustom, calls=%fused_computation.5.clone.1 | custom fusion | flops 8192 | bytes 1097740 | tf_op jit(solution)/shard_map/while/body/eval_jaxpr/scatter-add | solution.py:85
  221.6 12.4 %scatter_custom_fusion.9 = f32[4097,2]{1,0:T(8,128)S(1)} fusion(s32[2048]{0:T(1024)S(1)} %get-tuple-element.179, f32[]{:T(128)} %constant.23.clone.1..sunk, f32[2,2048]{0,1:T(8,128)} %get-tuple-element.178, f32[2,2048]{0,1:T(8,128)S(1)} %get-tuple-element.165), kind=kCustom, calls=%fused_computation.5.clone.1 | custom fusion | flops 8192 | bytes 1097740 | tf_op jit(solution)/shard_map/while/body/eval_jaxpr/scatter-add | solution.py:85
  246.5 12.4 %scatter_custom_fusion.9 = f32[4097,2]{1,0:T(8,128)S(1)} fusion(s32[2048]{0:T(1024)S(1)} %get-tuple-element.179, f32[]{:T(128)} %constant.23.clone.1..sunk, f32[2,2048]{0,1:T(8,128)} %get-tuple-element.178, f32[2,2048]{0,1:T(8,128)S(1)} %get-tuple-element.165), kind=kCustom, calls=%fused_computation.5.clone.1 | custom fusion | flops 8192 | bytes 1097740 | tf_op jit(solution)/shard_map/while/body/eval_jaxpr/scatter-add | solution.py:85
  270.9 12.4 %scatter_custom_fusion.9 = f32[4097,2]{1,0:T(8,128)S(1)} fusion(s32[2048]{0:T(1024)S(1)} %get-tuple-element.179, f32[]{:T(128)} %constant.23.clone.1..sunk, f32[2,2048]{0,1:T(8,128)} %get-tuple-element.178, f32[2,2048]{0,1:T(8,128)S(1)} %get-tuple-element.165), kind=kCustom, calls=%fused_computation.5.clone.1 | custom fusion | flops 8192 | bytes 1097740 | tf_op jit(solution)/shard_map/while/body/eval_jaxpr/scatter-add | solution.py:85
  296.8 12.4 %scatter_custom_fusion.9 = f32[4097,2]{1,0:T(8,128)S(1)} fusion(s32[2048]{0:T(1024)S(1)} %get-tuple-element.179, f32[]{:T(128)} %constant.23.clone.1..sunk, f32[2,2048]{0,1:T(8,128)} %get-tuple-element.178, f32[2,2048]{0,1:T(8,128)S(1)} %get-tuple-element.165), kind=kCustom, calls=%fused_computation.5.clone.1 | custom fusion | flops 8192 | bytes 1097740 | tf_op jit(solution)/shard_map/while/body/eval_jaxpr/scatter-add | solution.py:85
  321.1 12.4 %scatter_custom_fusion.9 = f32[4097,2]{1,0:T(8,128)S(1)} fusion(s32[2048]{0:T(1024)S(1)} %get-tuple-element.179, f32[]{:T(128)} %constant.23.clone.1..sunk, f32[2,2048]{0,1:T(8,128)} %get-tuple-element.178, f32[2,2048]{0,1:T(8,128)S(1)} %get-tuple-element.165), kind=kCustom, calls=%fused_computation.5.clone.1 | custom fusion | flops 8192 | bytes 1097740 | tf_op jit(solution)/shard_map/while/body/eval_jaxpr/scatter-add | solution.py:85
  347.8 6.2 %gather_fusion.1 = f32[1024]{0:T(1024)S(1)} fusion(f32[2048]{0:T(1024)S(1)} %add_divide_fusion, s32[1024]{0:T(1024)S(1)} %get-tuple-element.75), kind=kCustom, calls=%fused_computation.1 | custom fusion | bytes 12288 | tf_op jit(solution)/shard_map/gather | solution.py:139
  374.7 10.4 %all-to-all-start.1 = ((f32[32,4,8]{2,1,0:T(4,128)}), f32[32,4,8]{2,1,0:T(4,128)S(1)}, u32[]{:S(2)}, u32[]{:S(2)}) async-start(f32[32,4,8]{2,1,0:T(4,128)} %constant_dynamic-update-slice_fusion), calls=%async_computation.1 | async-start | bytes 131072 | tf_op jit(solution)/shard_map/all_to_all | solution.py:142
  395.6 3.9 all-to-all-start.2
  400.2 4.7 %all-to-all-done.2 = f32[4,1,256]{2,1,0:T(1,128)S(1)} async-done(((f32[4,1,256]{2,1,0:T(1,128)}), f32[4,1,256]{2,1,0:T(1,128)S(1)}, u32[]{:S(2)}, u32[]{:S(2)}) %all-to-all-start.2) | async-done | bytes 4128 | tf_op jit(solution)/shard_map/all_to_all | solution.py:140
  404.9 7.6 %scatter_custom_fusion.2 = f32[129]{0:T(256)S(1)} fusion(s32[1024]{0:T(1024)S(1)} %get-tuple-element.92, f32[1024]{0:T(1024)S(1)} %mul.247, f32[]{:T(128)} %constant.23.clone.1), kind=kCustom, calls=%fused_computation.142 | custom fusion | flops 1024 | bytes 520 | tf_op jit(solution)/shard_map/scatter-add | solution.py:157
  412.6 4.9 %fusion.5 = f32[48,64,128]{2,1,0:T(8,128)} fusion(f32[6,8,64,128]{3,2,1,0:T(8,128)} %copy.269, f32[6,8,64,128]{3,2,1,0:T(8,128)} %copy.268, f32[6,8,64,128]{3,2,1,0:T(8,128)} %copy.267, f32[6,8,64,128]{3,2,1,0:T(8,128)} %copy.266, f32[64,128]{1,0:T(8,128)S(1)} %multiply_exponential_fusion, f32[128]{0:T(128)S(1)} %get-tuple-element.86, ...), kind=kLoop, calls=%fused_computation.14 | loop fusion | flops 3145728 | bytes 7899136 | tf_op jit(solution)/shard_map/mul | solution.py:162
  (323 shorter events, 201.1 us)
Async XLA Ops:
  5.8 23.1 %copy-start.4 = (f32[48,64,128]{2,1,0:T(8,128)}, f32[48,64,128]{2,1,0:T(8,128)S(1)}, u32[]{:S(2)}) copy-start(f32[48,64,128]{2,1,0:T(8,128)S(1)} %get-tuple-element.70) | copy-start | bytes 4718596
  5.8 15.7 %copy-start.9 = (f32[4,48,48]{2,1,0:T(8,128)S(1)}, f32[4,48,48]{2,1,0:T(8,128)}, u32[]{:S(2)}) copy-start(f32[4,48,48]{2,1,0:T(8,128)} %param.20) | copy-start | bytes 110596
  11.0 26.0 %all-to-all-start = ((f32[128,3,1,8]{3,2,1,0:T(1,128)}), f32[128,3,1,8]{3,2,1,0:T(1,128)S(1)}, u32[]{:S(2)}, u32[]{:S(2)}) async-start(f32[128,3,1,8]{3,2,1,0:T(1,128)} %bitcast.27), calls=%async_computation | async-start | bytes 393216 | tf_op jit(solution)/shard_map/all_to_all | solution.py:27
  62.3 7.8 %collective-permute-start = (f32[2,2048]{1,0:T(2,128)S(1)}, f32[2,2048]{1,0:T(2,128)S(1)}, u32[]{:S(2)}, u32[]{:S(2)}) collective-permute-start(f32[2,2048]{1,0:T(2,128)S(1)} %copy.292), channel_id=1, source_target_pairs={{0,1},{1,2},{2,3},{3,4},{4,5},{5,6},{6,7},{7,8},{8,9},{9,10},{10,1... | collective-permute-start | bytes 49160 | tf_op jit(solution)/shard_map/while/body/eval_jaxpr/ppermute | solution.py:35
  85.0 5.2 %copy-start = (f32[2,2048]{0,1:T(8,128)S(1)}, f32[2,2048]{0,1:T(8,128)}, u32[]{:S(2)}) copy-start(f32[2,2048]{0,1:T(8,128)} %get-tuple-element.178) | copy-start | bytes 49156 | tf_op jit(solution)/shard_map/while
  86.7 9.3 %collective-permute-start = (f32[2,2048]{1,0:T(2,128)S(1)}, f32[2,2048]{1,0:T(2,128)S(1)}, u32[]{:S(2)}, u32[]{:S(2)}) collective-permute-start(f32[2,2048]{1,0:T(2,128)S(1)} %copy.292), channel_id=1, source_target_pairs={{0,1},{1,2},{2,3},{3,4},{4,5},{5,6},{6,7},{7,8},{8,9},{9,10},{10,1... | collective-permute-start | bytes 49160 | tf_op jit(solution)/shard_map/while/body/eval_jaxpr/ppermute | solution.py:35
  112.5 7.9 %collective-permute-start = (f32[2,2048]{1,0:T(2,128)S(1)}, f32[2,2048]{1,0:T(2,128)S(1)}, u32[]{:S(2)}, u32[]{:S(2)}) collective-permute-start(f32[2,2048]{1,0:T(2,128)S(1)} %copy.292), channel_id=1, source_target_pairs={{0,1},{1,2},{2,3},{3,4},{4,5},{5,6},{6,7},{7,8},{8,9},{9,10},{10,1... | collective-permute-start | bytes 49160 | tf_op jit(solution)/shard_map/while/body/eval_jaxpr/ppermute | solution.py:35
  135.2 5.3 %copy-start = (f32[2,2048]{0,1:T(8,128)S(1)}, f32[2,2048]{0,1:T(8,128)}, u32[]{:S(2)}) copy-start(f32[2,2048]{0,1:T(8,128)} %get-tuple-element.178) | copy-start | bytes 49156 | tf_op jit(solution)/shard_map/while
  136.9 9.4 %collective-permute-start = (f32[2,2048]{1,0:T(2,128)S(1)}, f32[2,2048]{1,0:T(2,128)S(1)}, u32[]{:S(2)}, u32[]{:S(2)}) collective-permute-start(f32[2,2048]{1,0:T(2,128)S(1)} %copy.292), channel_id=1, source_target_pairs={{0,1},{1,2},{2,3},{3,4},{4,5},{5,6},{6,7},{7,8},{8,9},{9,10},{10,1... | collective-permute-start | bytes 49160 | tf_op jit(solution)/shard_map/while/body/eval_jaxpr/ppermute | solution.py:35
  162.8 7.9 %collective-permute-start = (f32[2,2048]{1,0:T(2,128)S(1)}, f32[2,2048]{1,0:T(2,128)S(1)}, u32[]{:S(2)}, u32[]{:S(2)}) collective-permute-start(f32[2,2048]{1,0:T(2,128)S(1)} %copy.292), channel_id=1, source_target_pairs={{0,1},{1,2},{2,3},{3,4},{4,5},{5,6},{6,7},{7,8},{8,9},{9,10},{10,1... | collective-permute-start | bytes 49160 | tf_op jit(solution)/shard_map/while/body/eval_jaxpr/ppermute | solution.py:35
  185.5 5.0 %copy-start = (f32[2,2048]{0,1:T(8,128)S(1)}, f32[2,2048]{0,1:T(8,128)}, u32[]{:S(2)}) copy-start(f32[2,2048]{0,1:T(8,128)} %get-tuple-element.178) | copy-start | bytes 49156 | tf_op jit(solution)/shard_map/while
  187.1 9.1 %collective-permute-start = (f32[2,2048]{1,0:T(2,128)S(1)}, f32[2,2048]{1,0:T(2,128)S(1)}, u32[]{:S(2)}, u32[]{:S(2)}) collective-permute-start(f32[2,2048]{1,0:T(2,128)S(1)} %copy.292), channel_id=1, source_target_pairs={{0,1},{1,2},{2,3},{3,4},{4,5},{5,6},{6,7},{7,8},{8,9},{9,10},{10,1... | collective-permute-start | bytes 49160 | tf_op jit(solution)/shard_map/while/body/eval_jaxpr/ppermute | solution.py:35
  212.7 7.8 %collective-permute-start = (f32[2,2048]{1,0:T(2,128)S(1)}, f32[2,2048]{1,0:T(2,128)S(1)}, u32[]{:S(2)}, u32[]{:S(2)}) collective-permute-start(f32[2,2048]{1,0:T(2,128)S(1)} %copy.292), channel_id=1, source_target_pairs={{0,1},{1,2},{2,3},{3,4},{4,5},{5,6},{6,7},{7,8},{8,9},{9,10},{10,1... | collective-permute-start | bytes 49160 | tf_op jit(solution)/shard_map/while/body/eval_jaxpr/ppermute | solution.py:35
  237.1 8.4 %collective-permute-start = (f32[2,2048]{1,0:T(2,128)S(1)}, f32[2,2048]{1,0:T(2,128)S(1)}, u32[]{:S(2)}, u32[]{:S(2)}) collective-permute-start(f32[2,2048]{1,0:T(2,128)S(1)} %copy.292), channel_id=1, source_target_pairs={{0,1},{1,2},{2,3},{3,4},{4,5},{5,6},{6,7},{7,8},{8,9},{9,10},{10,1... | collective-permute-start | bytes 49160 | tf_op jit(solution)/shard_map/while/body/eval_jaxpr/ppermute | solution.py:35
  262.0 7.9 %collective-permute-start = (f32[2,2048]{1,0:T(2,128)S(1)}, f32[2,2048]{1,0:T(2,128)S(1)}, u32[]{:S(2)}, u32[]{:S(2)}) collective-permute-start(f32[2,2048]{1,0:T(2,128)S(1)} %copy.292), channel_id=1, source_target_pairs={{0,1},{1,2},{2,3},{3,4},{4,5},{5,6},{6,7},{7,8},{8,9},{9,10},{10,1... | collective-permute-start | bytes 49160 | tf_op jit(solution)/shard_map/while/body/eval_jaxpr/ppermute | solution.py:35
  284.8 5.2 %copy-start = (f32[2,2048]{0,1:T(8,128)S(1)}, f32[2,2048]{0,1:T(8,128)}, u32[]{:S(2)}) copy-start(f32[2,2048]{0,1:T(8,128)} %get-tuple-element.178) | copy-start | bytes 49156 | tf_op jit(solution)/shard_map/while
  286.4 9.4 %collective-permute-start = (f32[2,2048]{1,0:T(2,128)S(1)}, f32[2,2048]{1,0:T(2,128)S(1)}, u32[]{:S(2)}, u32[]{:S(2)}) collective-permute-start(f32[2,2048]{1,0:T(2,128)S(1)} %copy.292), channel_id=1, source_target_pairs={{0,1},{1,2},{2,3},{3,4},{4,5},{5,6},{6,7},{7,8},{8,9},{9,10},{10,1... | collective-permute-start | bytes 49160 | tf_op jit(solution)/shard_map/while/body/eval_jaxpr/ppermute | solution.py:35
  312.3 7.8 %collective-permute-start = (f32[2,2048]{1,0:T(2,128)S(1)}, f32[2,2048]{1,0:T(2,128)S(1)}, u32[]{:S(2)}, u32[]{:S(2)}) collective-permute-start(f32[2,2048]{1,0:T(2,128)S(1)} %copy.292), channel_id=1, source_target_pairs={{0,1},{1,2},{2,3},{3,4},{4,5},{5,6},{6,7},{7,8},{8,9},{9,10},{10,1... | collective-permute-start | bytes 49160 | tf_op jit(solution)/shard_map/while/body/eval_jaxpr/ppermute | solution.py:35
  335.0 5.3 %copy-start = (f32[2,2048]{0,1:T(8,128)S(1)}, f32[2,2048]{0,1:T(8,128)}, u32[]{:S(2)}) copy-start(f32[2,2048]{0,1:T(8,128)} %get-tuple-element.178) | copy-start | bytes 49156 | tf_op jit(solution)/shard_map/while
  336.6 9.4 %collective-permute-start = (f32[2,2048]{1,0:T(2,128)S(1)}, f32[2,2048]{1,0:T(2,128)S(1)}, u32[]{:S(2)}, u32[]{:S(2)}) collective-permute-start(f32[2,2048]{1,0:T(2,128)S(1)} %copy.292), channel_id=1, source_target_pairs={{0,1},{1,2},{2,3},{3,4},{4,5},{5,6},{6,7},{7,8},{8,9},{9,10},{10,1... | collective-permute-start | bytes 49160 | tf_op jit(solution)/shard_map/while/body/eval_jaxpr/ppermute | solution.py:35
  347.8 37.3 %copy-start.5 = (f32[48,64,128]{2,1,0:T(8,128)S(1)}, f32[48,64,128]{2,1,0:T(8,128)}, u32[]{:S(2)}) copy-start(f32[48,64,128]{2,1,0:T(8,128)} %copy-done.4) | copy-start | bytes 4718596
  374.7 20.2 %all-to-all-start.1 = ((f32[32,4,8]{2,1,0:T(4,128)}), f32[32,4,8]{2,1,0:T(4,128)S(1)}, u32[]{:S(2)}, u32[]{:S(2)}) async-start(f32[32,4,8]{2,1,0:T(4,128)} %constant_dynamic-update-slice_fusion), calls=%async_computation.1 | async-start | bytes 131072 | tf_op jit(solution)/shard_map/all_to_all | solution.py:142
  395.6 9.2 %all-to-all-start.2 = ((f32[4,1,256]{2,1,0:T(1,128)}), f32[4,1,256]{2,1,0:T(1,128)S(1)}, u32[]{:S(2)}, u32[]{:S(2)}) async-start(f32[4,1,256]{2,1,0:T(1,128)} %all_to_all.16), calls=%async_computation.2 | async-start | bytes 8192 | tf_op jit(solution)/shard_map/all_to_all | solution.py:140
  412.5 5.0 %copy-start.20 = (f32[128]{0:T(128)}, f32[128]{0:T(128)S(1)}, u32[]{:S(2)}) copy-start(f32[128]{0:T(128)S(1)} %slice.114) | copy-start | bytes 1540
  (45 other events, 107.7 us)
